TPU v7x, 512 devices: a whole 4x4x16 slice. The times are simulated.
512 devices in a mesh: row: 64 (over z, y), col: 8 (over x, core).
Axes of the slice: x: 4, y: 4, z: 16, core: 2. Of those that a mesh axis runs over, the one named last changes fastest.
Arguments:
- acts: bfloat16 [8192, 8192], P('row'), may hold values from -22 to 22
- out_grads: bfloat16 [8192, 4096], P('row', 'col'), may hold values from -0.099436891 to 0.099436891
- weight: float32 [8192, 4096], P('row', 'col'), may hold values from -30 to 30
- row_state: float32 [8192], P('row'), may hold values from 0.002 to 2
- col_state: float32 [4096], P('col'), may hold values from 0.01 to 0.3
Outputs:
- new_weight: float32 [8192, 4096], P('row', 'col')
- update: float32 [8192, 4096], P('row', 'col')
- row_moment: float32 [8192], P('row')
- col_moment: float32 [4096], P('col')
All inputs are finite; a program needn't handle non-finite values.
Results may differ from a plain program's by a relative error of at most 0.0003.
Values may be sent and summed in bfloat16 or wider, within the bound.
A program may use at most 64 MiB of HBM per device.

v0:
```python
import jax
import jax.numpy as jnp
from jax import lax
from jax.sharding import Mesh
from jax.sharding import PartitionSpec as P

Z, Y = ("row_0", "row_1")
ROW = (Z, Y)
COL = ("col_0", "col_1")
decay_rate = 0.85
floor_eps = 1e-30
relative_rate = 0.05


def per_device(acts, out_grads, weight, row_state, col_state):
    n_row = lax.axis_size(ROW)
    n_z = lax.axis_size(Z)
    n_y = lax.axis_size(Y)
    n_col = lax.axis_size(COL)
    tok_dev = acts.shape[0]
    width = acts.shape[1]
    cols_here = out_grads.shape[1]
    cols_all = cols_here * n_col
    share_rows = tok_dev // n_col
    own_rows = lax.dynamic_slice_in_dim(acts, lax.axis_index(COL) * share_rows, share_rows, 0)
    arrived = lax.all_to_all(own_rows, Z, split_axis=1, concat_axis=0, tiled=True)
    columns = lax.all_gather(
        arrived.reshape(n_z, share_rows, width // n_z), COL, axis=1, tiled=True
    )
    columns = columns.reshape(n_z * tok_dev, width // n_z)
    gathered = lax.all_gather(out_grads, Z, axis=0, tiled=True)
    partial = lax.dot_general(
        columns, gathered, (((0,), (0,)), ((), ())), preferred_element_type=jnp.float32
    )
    gradient = lax.psum_scatter(partial, Y, scatter_dimension=0, tiled=True)
    squares = gradient * gradient + floor_eps
    row_squares = jnp.sum(squares, axis=1)
    col_squares = jnp.sum(squares, axis=0)
    weight_part = jnp.sum(weight * weight)
    row_total = lax.psum(row_squares, COL)
    row_moment = decay_rate * row_state + (1.0 - decay_rate) * (row_total / cols_all)
    scaled = gradient * lax.rsqrt(row_moment)[:, None]
    stacked = jnp.concatenate([col_squares, jnp.sum(scaled * scaled, axis=0)])
    stacked = lax.psum(stacked, ROW)
    col_total, scaled_total = (stacked[:cols_here], stacked[cols_here:])
    col_moment = decay_rate * col_state + (1.0 - decay_rate) * (col_total / width)
    unclipped = gradient * lax.rsqrt(row_moment[:, None] * col_moment[None, :])
    update_total = lax.psum(jnp.sum(scaled_total / col_moment), COL)
    weight_total = lax.psum(weight_part, ROW + COL)
    count_all = width * cols_all
    clip_factor = jnp.maximum(1.0, jnp.sqrt(update_total / count_all))
    update = unclipped / clip_factor
    step_size = relative_rate * jnp.sqrt(weight_total / count_all + 1e-06)
    new_weight = weight - step_size * update
    return (new_weight, update, row_moment, col_moment)


def solution(mesh):
    finer = Mesh(mesh.devices.reshape(16, 4, 4, 2), (Z, Y) + COL)
    placed = (P(ROW, None), P(ROW, COL), P(ROW, COL), P(ROW), P(COL))
    return jax.shard_map(
        per_device,
        mesh=finer,
        in_specs=placed,
        out_specs=(P(ROW, COL), P(ROW, COL), P(ROW), P(COL)),
        check_vma=False,
    )
```

profile of v0, /device:TPU:1, one launch (start us, length us, event | category | flops | bytes accessed | tf_op | source)
XLA Modules:
  0.0 432.5 jit_solution(11988476071683671557)
XLA Ops:
  7.2 0.0 copy-start
  7.2 0.0 all-gather.3.cloned.1.call-start
  7.2 1.5 copy-done
  8.8 28.7 %all_to_all.16 = bf16[16,16,512]{2,0,1:T(8,128)(2,1)S(1)} all-to-all(bf16[16,16,512]{2,0,1:T(8,128)(2,1)S(1)} %bitcast.10), channel_id=1, replica_groups=mesh['row_0'=16,'row_1'=4,'col_0'=4,'col_1'=2] {'row_0'}, dimensions={1} | all-to-all | bytes 524288 | tf_op jit(solution)/shard_map/all_to_all | solution.py:26
  37.5 0.9 copy.11
  38.3 0.0 all-gather.3.cloned.1.call-update
  38.4 0.0 all-gather.5.cloned.1.call-start
  38.4 0.7 all-gather.5.cloned.1.call-update
  39.1 0.0 reduce-scatter.2.cloned.1.call-start
  39.2 33.2 %all-gather.3.cloned.1.call-done = bf16[16,128,512]{2,0,1:T(8,128)(2,1)} async-done(((bf16[16,16,512]{2,0,1:T(8,128)(2,1)}), bf16[16,128,512]{2,0,1:T(8,128)(2,1)}) %all-gather.3.cloned.1.call-update) | async-done | bytes 2097168 | tf_op jit(solution)/shard_map/all_gather | solution.py:27
  72.3 4.0 copy.12
  76.4 62.1 %all-gather.5.cloned.1.call-done = bf16[2048,512]{1,0:T(8,128)(2,1)} async-done(((bf16[128,512]{1,0:T(8,128)(2,1)}), bf16[2048,512]{1,0:T(8,128)(2,1)}) %all-gather.5.cloned.1.call-update) | async-done | bytes 2097168 | tf_op jit(solution)/shard_map/all_gather | solution.py:31
  138.5 0.0 copy-start.1
  138.5 0.0 copy-start.5
  138.5 0.0 copy-start.4
  138.5 4.5 %fusion.4 = f32[512,512]{1,0:T(8,128)} fusion(bf16[2048,512]{1,0:T(8,128)(2,1)} %bitcast.8, bf16[2048,512]{1,0:T(8,128)(2,1)} %all-gather.5.cloned.1.call-done), kind=kOutput, calls=%fused_computation.15 | convolution fusion | flops 1073741824 | bytes 5242880 | tf_op jit(solution)/shard_map/dot_general | solution.py:32
  143.0 0.0 reduce-scatter.2.cloned.1.call-update
  143.0 0.0 copy-done.1
  143.0 0.7 multiply_reduce_fusion.1
  143.7 110.9 %psum.28 = f32[]{:T(128)} all-reduce(f32[]{:T(128)} %multiply_reduce_fusion.1), channel_id=1, replica_groups=mesh['row_0'=16,'row_1'=4,'col_0'=4,'col_1'=2] {'row_0','row_1','col_0',..., use_global_device_ids=true, to_apply=%region_1.0 | all-reduce | flops 1 | bytes 8 | tf_op jit(solution)/shard_map/psum | solution.py:49
  255.2 0.0 reduce-scatter.2.cloned.1.call-done
  255.3 1.1 fusion.1
  256.3 12.4 %psum.29 = f32[128]{0:T(128)S(1)} all-reduce(f32[128]{0:T(128)S(1)} %fusion.1), channel_id=1, replica_groups=mesh['row_0'=16,'row_1'=4,'col_0'=4,'col_1'=2] {'col_0','col_1'}, use_global_device_ids=true, to_apply=%region_4.0 | all-reduce | flops 128 | bytes 1024 | tf_op jit(solution)/shard_map/psum | solution.py:40
  268.8 0.0 copy-done.5
  268.8 0.0 copy-start.3
  268.8 1.1 fusion
  269.9 112.1 %psum.30 = f32[1024]{0:T(1024)S(1)} all-reduce(f32[1024]{0:T(1024)S(1)} %pad_maximum_fusion), channel_id=1, replica_groups=mesh['row_0'=16,'row_1'=4,'col_0'=4,'col_1'=2] {'row_0','row_1'}, use_global_device_ids=true, to_apply=%region_7.0 | all-reduce | flops 1024 | bytes 8192 | tf_op jit(solution)/shard_map/psum | solution.py:44
  382.0 0.0 copy-done.4
  382.0 0.6 fusion.2
  382.6 0.0 copy-start.2
  382.6 40.8 %psum.31 = f32[]{:T(128)} all-reduce(f32[]{:T(128)} %get-tuple-element.8), channel_id=1, replica_groups=mesh['row_0'=16,'row_1'=4,'col_0'=4,'col_1'=2] {'col_0','col_1'}, use_global_device_ids=true, to_apply=%region_9.0 | all-reduce | flops 1 | bytes 8 | tf_op jit(solution)/shard_map/psum | solution.py:48
  424.1 1.9 multiply_subtract_fusion
  425.9 0.0 copy-done.3
  426.0 0.0 copy-done.2
  (4 shorter events, 0.1 us)
Async XLA Ops:
  7.2 1.6 copy-start
  7.2 65.1 %all-gather.3.cloned.1.call-start = ((), (), s32[]{:S(2)}) async-start(), calls=%async_computation.2 | async-start | bytes 2359296 | tf_op jit(solution)/shard_map/all_gather | solution.py:27
  38.4 100.1 %all-gather.5.cloned.1.call-start = ((), (), s32[]{:S(2)}) async-start(), calls=%async_computation.3 | async-start | bytes 2228224 | tf_op jit(solution)/shard_map/all_gather | solution.py:31
  39.1 216.1 %reduce-scatter.2.cloned.1.call-start = ((), (), s32[]{:S(2)}) async-start(), calls=%async_computation.4 | async-start | bytes 1310720 | tf_op jit(solution)/shard_map/reduce_scatter | solution.py:35
  138.5 4.5 %copy-start.1 = (f32[128,512]{1,0:T(8,128)S(1)}, f32[128,512]{1,0:T(8,128)}, u32[]{:S(2)}) copy-start(f32[128,512]{1,0:T(8,128)} %param.7) | copy-start | bytes 786436
  138.5 130.3 %copy-start.5 = (f32[128]{0:T(128)S(1)}, f32[128]{0:T(128)}, u32[]{:S(2)}) copy-start(f32[128]{0:T(128)} %param.8) | copy-start | bytes 1540
  138.5 243.5 %copy-start.4 = (f32[512]{0:T(512)S(1)}, f32[512]{0:T(512)}, u32[]{:S(2)}) copy-start(f32[512]{0:T(512)} %param.9) | copy-start | bytes 6148
  268.8 157.2 %copy-start.3 = (f32[128]{0:T(128)}, f32[128]{0:T(128)S(1)}, u32[]{:S(2)}) copy-start(f32[128]{0:T(128)S(1)} %get-tuple-element.11) | copy-start | bytes 1540
  382.6 43.4 %copy-start.2 = (f32[512]{0:T(512)}, f32[512]{0:T(512)S(1)}, u32[]{:S(2)}) copy-start(f32[512]{0:T(512)S(1)} %get-tuple-element.9) | copy-start | bytes 6148
Sparse Core Ops, SparseCore 0:
  38.5 33.7 all-gather.2
  74.4 64.0 all-gather.4
  143.1 36.4 reduce-scatter.1
where the time goes:
time: 433 us; the launch traced here: 432 us
  blocking collectives  305 us (70%)
  waiting for transfers between devices  96 us (22%)
  between operations  15.2 us (4%)
  local copies, waits for them, and re-layouts  6.49 us (1%)
  other arithmetic  5.28 us (1%)
  matrix products  4.51 us (1%)
    psum x1, blocking collectives, per_device(): stacked = lax.psum(stacked, ROW)  112 us
    psum x1, blocking collectives, per_device(): weight_total = lax.psum(weight_part, ROW + COL)  111 us
    all_gather x1, waiting for transfers between devices, per_device(): gathered = lax.all_gather(out_grads, Z, axis=0, tiled=True)  62.1 us
    psum x1, blocking collectives, per_device(): update_total = lax.psum(jnp.sum(scaled_total / col_moment), COL)  40.8 us
    all_gather x1, waiting for transfers between devices, per_device(): lax.all_gather(arrived.reshape(n_z, share_rows, width // n_z), COL, axis=...  33.2 us
    all_to_all x1, blocking collectives, per_device(): lax.all_to_all(own_rows, Z, split_axis=1, concat_axis=0, tiled=True)  28.7 us
    psum x1, blocking collectives, per_device(): row_total = lax.psum(row_squares, COL)  12.4 us
  transfers between devices with their start and end apart: 3, of which 2 were waited for; matrix products, arithmetic and copies ran while one was open for 1% of the time, Pallas kernels for 0%

commit v1 on v0

--- a/solution.py
+++ b/solution.py
@@ -41,7 +41,10 @@
     row_moment = decay_rate * row_state + (1.0 - decay_rate) * (row_total / cols_all)
     scaled = gradient * lax.rsqrt(row_moment)[:, None]
     stacked = jnp.concatenate([col_squares, jnp.sum(scaled * scaled, axis=0)])
-    stacked = lax.psum(stacked, ROW)
+    direct_views_by_axis = lambda u_in, mesh_dim, group_axis: lax.psum(
+        lax.psum(u_in, mesh_dim), group_axis
+    )
+    stacked = direct_views_by_axis(stacked, Y, Z)
     col_total, scaled_total = (stacked[:cols_here], stacked[cols_here:])
     col_moment = decay_rate * col_state + (1.0 - decay_rate) * (col_total / width)
     unclipped = gradient * lax.rsqrt(row_moment[:, None] * col_moment[None, :])

time: 433 us -> 330 us (0.76)
  blocking collectives: 305 us -> 202 us
    psum x1 -> x2, blocking collectives: 112 us -> 28.6 us  [the longest x1 20.3 us: per_device(): lax.psum(lax.psum(u_in, mesh_dim), group_axis)]
    psum x1, blocking collectives: 40.8 us -> 21.7 us  [per_device(): update_total = lax.psum(jnp.sum(scaled_total / col_moment), COL)]
where the time goes in v1:
time: 330 us
  blocking collectives  202 us (61%)
  waiting for transfers between devices  96 us (29%)
  between operations  15.2 us (5%)
  local copies, waits for them, and re-layouts  6.49 us (2%)
  other arithmetic  5.28 us (2%)
  matrix products  4.51 us (1%)
    psum x1, blocking collectives, per_device(): weight_total = lax.psum(weight_part, ROW + COL)  111 us
    all_gather x1, waiting for transfers between devices, per_device(): gathered = lax.all_gather(out_grads, Z, axis=0, tiled=True)  62.1 us
    all_gather x1, waiting for transfers between devices, per_device(): lax.all_gather(arrived.reshape(n_z, share_rows, width // n_z), COL, axis=...  33.2 us
    all_to_all x1, blocking collectives, per_device(): lax.all_to_all(own_rows, Z, split_axis=1, concat_axis=0, tiled=True)  28.7 us
    psum x1, blocking collectives, per_device(): update_total = lax.psum(jnp.sum(scaled_total / col_moment), COL)  21.7 us
    psum x1, blocking collectives, per_device(): lax.psum(lax.psum(u_in, mesh_dim), group_axis)  20.3 us
    psum x1, blocking collectives, per_device(): row_total = lax.psum(row_squares, COL)  12.4 us
    psum x1, blocking collectives, per_device(): lax.psum(u_in, mesh_dim)  8.27 us
  transfers between devices with their start and end apart: 3, of which 2 were waited for; matrix products, arithmetic and copies ran while one was open for 1% of the time, Pallas kernels for 0%

profile of v1, /device:TPU:1, one launch (start us, length us, event | category | flops | bytes accessed | tf_op | source)
XLA Modules:
  0.0 329.9 jit_solution(11088789163010058334)
XLA Ops:
  7.2 0.0 copy-start
  7.2 0.0 all-gather.3.cloned.1.call-start
  7.2 1.5 copy-done
  8.8 28.7 %all_to_all.16 = bf16[16,16,512]{2,0,1:T(8,128)(2,1)S(1)} all-to-all(bf16[16,16,512]{2,0,1:T(8,128)(2,1)S(1)} %bitcast.10), channel_id=1, replica_groups=mesh['row_0'=16,'row_1'=4,'col_0'=4,'col_1'=2] {'row_0'}, dimensions={1} | all-to-all | bytes 524288 | tf_op jit(solution)/shard_map/all_to_all | solution.py:26
  37.5 0.9 copy.11
  38.3 0.0 all-gather.3.cloned.1.call-update
  38.4 0.0 all-gather.5.cloned.1.call-start
  38.4 0.7 all-gather.5.cloned.1.call-update
  39.1 0.0 reduce-scatter.2.cloned.1.call-start
  39.2 33.2 %all-gather.3.cloned.1.call-done = bf16[16,128,512]{2,0,1:T(8,128)(2,1)} async-done(((bf16[16,16,512]{2,0,1:T(8,128)(2,1)}), bf16[16,128,512]{2,0,1:T(8,128)(2,1)}) %all-gather.3.cloned.1.call-update) | async-done | bytes 2097168 | tf_op jit(solution)/shard_map/all_gather | solution.py:27
  72.3 4.0 %copy.12 = bf16[16,128,512]{2,1,0:T(8,128)(2,1)} copy(bf16[16,128,512]{2,0,1:T(8,128)(2,1)} %all-gather.3.cloned.1.call-done) | data formatting | bytes 4194304 | tf_op jit(solution)/shard_map/all_gather | solution.py:27
  76.4 62.1 %all-gather.5.cloned.1.call-done = bf16[2048,512]{1,0:T(8,128)(2,1)} async-done(((bf16[128,512]{1,0:T(8,128)(2,1)}), bf16[2048,512]{1,0:T(8,128)(2,1)}) %all-gather.5.cloned.1.call-update) | async-done | bytes 2097168 | tf_op jit(solution)/shard_map/all_gather | solution.py:31
  138.5 0.0 copy-start.1
  138.5 0.0 copy-start.5
  138.5 0.0 copy-start.4
  138.5 4.5 %fusion.4 = f32[512,512]{1,0:T(8,128)} fusion(bf16[2048,512]{1,0:T(8,128)(2,1)} %bitcast.8, bf16[2048,512]{1,0:T(8,128)(2,1)} %all-gather.5.cloned.1.call-done), kind=kOutput, calls=%fused_computation.15 | convolution fusion | flops 1073741824 | bytes 5242880 | tf_op jit(solution)/shard_map/dot_general | solution.py:32
  143.0 0.0 reduce-scatter.2.cloned.1.call-update
  143.0 0.0 copy-done.1
  143.0 0.7 multiply_reduce_fusion.1
  143.7 110.9 %psum.35 = f32[]{:T(128)} all-reduce(f32[]{:T(128)} %multiply_reduce_fusion.1), channel_id=1, replica_groups=mesh['row_0'=16,'row_1'=4,'col_0'=4,'col_1'=2] {'row_0','row_1','col_0',..., use_global_device_ids=true, to_apply=%region_1.0 | all-reduce | flops 1 | bytes 8 | tf_op jit(solution)/shard_map/psum | solution.py:52
  255.2 0.0 reduce-scatter.2.cloned.1.call-done
  255.3 1.1 fusion.1
  256.3 12.4 %psum.36 = f32[128]{0:T(128)S(1)} all-reduce(f32[128]{0:T(128)S(1)} %fusion.1), channel_id=1, replica_groups=mesh['row_0'=16,'row_1'=4,'col_0'=4,'col_1'=2] {'col_0','col_1'}, use_global_device_ids=true, to_apply=%region_4.0 | all-reduce | flops 128 | bytes 1024 | tf_op jit(solution)/shard_map/psum | solution.py:40
  268.8 0.0 copy-done.5
  268.8 0.0 copy-start.3
  268.8 1.1 fusion
  269.9 8.3 %psum.37 = f32[1024]{0:T(1024)S(1)} all-reduce(f32[1024]{0:T(1024)S(1)} %pad_maximum_fusion), channel_id=1, replica_groups=mesh['row_0'=16,'row_1'=4,'col_0'=4,'col_1'=2] {'row_1'}, use_global_device_ids=true, to_apply=%region_7.0 | all-reduce | flops 1024 | bytes 8192 | tf_op jit(solution)/shard_map/psum | solution.py:45
  278.1 20.3 %psum.38 = f32[1024]{0:T(1024)S(1)} all-reduce(f32[1024]{0:T(1024)S(1)} %psum.37), channel_id=1, replica_groups=mesh['row_0'=16,'row_1'=4,'col_0'=4,'col_1'=2] {'row_0'}, use_global_device_ids=true, to_apply=%region_8.0 | all-reduce | flops 1024 | bytes 8192 | tf_op jit(solution)/shard_map/psum | solution.py:44
  298.4 0.0 copy-done.4
  298.4 0.6 fusion.2
  299.0 0.0 copy-start.2
  299.0 21.7 %psum.39 = f32[]{:T(128)} all-reduce(f32[]{:T(128)} %get-tuple-element.8), channel_id=1, replica_groups=mesh['row_0'=16,'row_1'=4,'col_0'=4,'col_1'=2] {'col_0','col_1'}, use_global_device_ids=true, to_apply=%region_10.0 | all-reduce | flops 1 | bytes 8 | tf_op jit(solution)/shard_map/psum | solution.py:51
  321.5 1.9 multiply_subtract_fusion
  323.3 0.0 copy-done.3
  323.3 0.0 copy-done.2
  (4 shorter events, 0.1 us)
Async XLA Ops:
  7.2 1.6 copy-start
  7.2 65.1 %all-gather.3.cloned.1.call-start = ((), (), s32[]{:S(2)}) async-start(), calls=%async_computation.2 | async-start | bytes 2359296 | tf_op jit(solution)/shard_map/all_gather | solution.py:27
  38.4 100.1 %all-gather.5.cloned.1.call-start = ((), (), s32[]{:S(2)}) async-start(), calls=%async_computation.3 | async-start | bytes 2228224 | tf_op jit(solution)/shard_map/all_gather | solution.py:31
  39.1 216.1 %reduce-scatter.2.cloned.1.call-start = ((), (), s32[]{:S(2)}) async-start(), calls=%async_computation.4 | async-start | bytes 1310720 | tf_op jit(solution)/shard_map/reduce_scatter | solution.py:35
  138.5 4.5 %copy-start.1 = (f32[128,512]{1,0:T(8,128)S(1)}, f32[128,512]{1,0:T(8,128)}, u32[]{:S(2)}) copy-start(f32[128,512]{1,0:T(8,128)} %param.7) | copy-start | bytes 786436
  138.5 130.3 %copy-start.5 = (f32[128]{0:T(128)S(1)}, f32[128]{0:T(128)}, u32[]{:S(2)}) copy-start(f32[128]{0:T(128)} %param.8) | copy-start | bytes 1540
  138.5 160.0 %copy-start.4 = (f32[512]{0:T(512)S(1)}, f32[512]{0:T(512)}, u32[]{:S(2)}) copy-start(f32[512]{0:T(512)} %param.9) | copy-start | bytes 6148
  268.8 54.6 %copy-start.3 = (f32[128]{0:T(128)}, f32[128]{0:T(128)S(1)}, u32[]{:S(2)}) copy-start(f32[128]{0:T(128)S(1)} %get-tuple-element.11) | copy-start | bytes 1540
  299.0 24.3 %copy-start.2 = (f32[512]{0:T(512)}, f32[512]{0:T(512)S(1)}, u32[]{:S(2)}) copy-start(f32[512]{0:T(512)S(1)} %get-tuple-element.9) | copy-start | bytes 6148
Sparse Core Ops, SparseCore 0:
  38.5 33.7 all-gather.2
  74.4 64.0 all-gather.4
  143.1 36.4 reduce-scatter.1

commit v2 on v0

--- a/solution.py
+++ b/solution.py
@@ -23,7 +23,10 @@
     cols_all = cols_here * n_col
     share_rows = tok_dev // n_col
     own_rows = lax.dynamic_slice_in_dim(acts, lax.axis_index(COL) * share_rows, share_rows, 0)
-    arrived = lax.all_to_all(own_rows, Z, split_axis=1, concat_axis=0, tiled=True)
+    devices = lax.axis_size(Z)
+    blocks = jnp.stack(jnp.split(own_rows, devices, axis=1), axis=0)
+    blocks = lax.all_to_all(blocks, Z, split_axis=0, concat_axis=0)
+    arrived = jnp.concatenate(blocks, axis=0)
     columns = lax.all_gather(
         arrived.reshape(n_z, share_rows, width // n_z), COL, axis=1, tiled=True
     )

time: 433 us -> 417 us (0.963)
  waiting for transfers between devices: 96 us -> 74.4 us
  local copies, waits for them, and re-layouts: 6.49 us -> 11.5 us
    all_gather x1, waiting for transfers between devices: 62.1 us -> 34.5 us  [per_device(): gathered = lax.all_gather(out_grads, Z, axis=0, tiled=True)]
    unnamed x12 -> x25, local copies, waits for them, and re-layouts: 1.56 us -> 10.8 us
    all_gather x1, waiting for transfers between devices: 33.2 us -> 39.2 us  [per_device(): lax.all_gather(arrived.reshape(n_z, share_rows, width // n_z), COL, axis=...]
    psum x1, blocking collectives: 111 us -> 105 us  [per_device(): weight_total = lax.psum(weight_part, ROW + COL)]
    all_to_all x1, blocking collectives: 28.7 us -> 34.2 us  [per_device(): blocks = lax.all_to_all(blocks, Z, split_axis=0, concat_axis=0)]
  transfers between devices with their start and end apart: 3 -> 3, of which waited for: 2 -> 2; matrix products, arithmetic and copies ran while one was open for 1% -> 3% of each run, Pallas kernels for 0% -> 0%
where the time goes in v2:
time: 417 us; the launch traced here: 416 us
  blocking collectives  305 us (73%)
  waiting for transfers between devices  74.4 us (18%)
  between operations  15.2 us (4%)
  local copies, waits for them, and re-layouts  11.5 us (3%)
  other arithmetic  5.28 us (1%)
  matrix products  4.51 us (1%)
    psum x1, blocking collectives, per_device(): stacked = lax.psum(stacked, ROW)  113 us
    psum x1, blocking collectives, per_device(): weight_total = lax.psum(weight_part, ROW + COL)  105 us
    psum x1, blocking collectives, per_device(): update_total = lax.psum(jnp.sum(scaled_total / col_moment), COL)  40.6 us
    all_gather x1, waiting for transfers between devices, per_device(): lax.all_gather(arrived.reshape(n_z, share_rows, width // n_z), COL, axis=...  39.2 us
    all_gather x1, waiting for transfers between devices, per_device(): gathered = lax.all_gather(out_grads, Z, axis=0, tiled=True)  34.5 us
    all_to_all x1, blocking collectives, per_device(): blocks = lax.all_to_all(blocks, Z, split_axis=0, concat_axis=0)  34.2 us
    psum x1, blocking collectives, per_device(): row_total = lax.psum(row_squares, COL)  12.4 us
    unnamed x25, local copies, waits for them, and re-layouts  10.8 us
  transfers between devices with their start and end apart: 3, of which 2 were waited for; matrix products, arithmetic and copies ran while one was open for 3% of the time, Pallas kernels for 0%

profile of v2, /device:TPU:1, one launch (start us, length us, event | category | flops | bytes accessed | tf_op | source)
XLA Modules:
  0.0 415.9 jit_solution(7228155236273388175)
XLA Ops:
  7.2 0.0 all-gather.5.cloned.1.call-start
  7.2 0.7 all-gather.5.cloned.1.call-update
  7.9 0.0 all-gather.3.cloned.1.call-start
  8.0 0.7 constant_dynamic-update-slice_fusion.15
  8.7 0.7 constant_dynamic-update-slice_fusion.14
  9.4 0.7 constant_dynamic-update-slice_fusion.13
  10.1 0.7 constant_dynamic-update-slice_fusion.12
  10.8 0.7 constant_dynamic-update-slice_fusion.11
  11.6 0.7 constant_dynamic-update-slice_fusion.10
  12.3 0.7 constant_dynamic-update-slice_fusion.9
  13.0 0.7 constant_dynamic-update-slice_fusion.8
  13.7 0.7 constant_dynamic-update-slice_fusion.7
  14.4 0.7 constant_dynamic-update-slice_fusion.6
  15.2 0.7 constant_dynamic-update-slice_fusion.5
  15.9 0.7 constant_dynamic-update-slice_fusion.4
  16.6 0.7 constant_dynamic-update-slice_fusion.3
  17.3 0.7 constant_dynamic-update-slice_fusion.2
  18.0 0.7 constant_dynamic-update-slice_fusion.1
  18.7 0.7 constant_dynamic-update-slice_fusion
  19.5 34.2 %all_to_all.5 = bf16[16,16,512]{2,1,0:T(8,128)(2,1)} all-to-all(bf16[16,16,512]{2,1,0:T(8,128)(2,1)S(1)} %constant_dynamic-update-slice_fusion), channel_id=1, replica_groups=mesh['row_0'=16,'row_1'=4,'col_0'=4,'col_1'=2] {'row_0'}, dimensions={0} | all-to-all | bytes 524288 | tf_op jit(solution)/shard_map/all_to_all | solution.py:28
  53.6 0.0 all-gather.3.cloned.1.call-update
  53.6 0.0 reduce-scatter.2.cloned.1.call-start
  53.7 34.5 %all-gather.5.cloned.1.call-done = bf16[2048,512]{1,0:T(8,128)(2,1)} async-done(((bf16[128,512]{1,0:T(8,128)(2,1)}), bf16[2048,512]{1,0:T(8,128)(2,1)}) %all-gather.5.cloned.1.call-update) | async-done | bytes 2097168 | tf_op jit(solution)/shard_map/all_gather | solution.py:34
  88.2 39.2 %all-gather.3.cloned.1.call-done = bf16[16,128,512]{2,1,0:T(8,128)(2,1)} async-done(((bf16[16,16,512]{2,1,0:T(8,128)(2,1)}), bf16[16,128,512]{2,1,0:T(8,128)(2,1)}) %all-gather.3.cloned.1.call-update) | async-done | bytes 2097168 | tf_op jit(solution)/shard_map/all_gather | solution.py:30
  127.4 0.0 copy-start
  127.4 0.0 copy-start.4
  127.4 0.0 copy-start.3
  127.4 4.5 %fusion.4 = f32[512,512]{1,0:T(8,128)} fusion(bf16[2048,512]{1,0:T(8,128)(2,1)} %bitcast.67, bf16[2048,512]{1,0:T(8,128)(2,1)} %all-gather.5.cloned.1.call-done), kind=kOutput, calls=%fused_computation.45 | convolution fusion | flops 1073741824 | bytes 5242880 | tf_op jit(solution)/shard_map/dot_general | solution.py:35
  131.9 0.0 reduce-scatter.2.cloned.1.call-update
  132.0 0.0 copy-done
  132.0 0.7 multiply_reduce_fusion.1
  132.6 104.9 %psum.28 = f32[]{:T(128)} all-reduce(f32[]{:T(128)} %multiply_reduce_fusion.1), channel_id=1, replica_groups=mesh['row_0'=16,'row_1'=4,'col_0'=4,'col_1'=2] {'row_0','row_1','col_0',..., use_global_device_ids=true, to_apply=%region_1.0 | all-reduce | flops 1 | bytes 8 | tf_op jit(solution)/shard_map/psum | solution.py:52
  238.2 0.0 reduce-scatter.2.cloned.1.call-done
  238.3 1.1 fusion.1
  239.3 12.4 %psum.29 = f32[128]{0:T(128)S(1)} all-reduce(f32[128]{0:T(128)S(1)} %fusion.1), channel_id=1, replica_groups=mesh['row_0'=16,'row_1'=4,'col_0'=4,'col_1'=2] {'col_0','col_1'}, use_global_device_ids=true, to_apply=%region_4.0 | all-reduce | flops 128 | bytes 1024 | tf_op jit(solution)/shard_map/psum | solution.py:43
  251.8 0.0 copy-done.4
  251.8 0.0 copy-start.2
  251.8 1.1 fusion
  252.9 112.7 %psum.30 = f32[1024]{0:T(1024)S(1)} all-reduce(f32[1024]{0:T(1024)S(1)} %pad_maximum_fusion), channel_id=1, replica_groups=mesh['row_0'=16,'row_1'=4,'col_0'=4,'col_1'=2] {'row_0','row_1'}, use_global_device_ids=true, to_apply=%region_7.0 | all-reduce | flops 1024 | bytes 8192 | tf_op jit(solution)/shard_map/psum | solution.py:47
  365.5 0.0 copy-done.3
  365.5 0.6 fusion.2
  366.2 0.0 copy-start.1
  366.2 40.6 %psum.31 = f32[]{:T(128)} all-reduce(f32[]{:T(128)} %get-tuple-element.8), channel_id=1, replica_groups=mesh['row_0'=16,'row_1'=4,'col_0'=4,'col_1'=2] {'col_0','col_1'}, use_global_device_ids=true, to_apply=%region_9.0 | all-reduce | flops 1 | bytes 8 | tf_op jit(solution)/shard_map/psum | solution.py:51
  407.5 1.9 multiply_subtract_fusion
  409.4 0.0 copy-done.2
  409.4 0.0 copy-done.1
  (2 shorter events, 0.0 us)
Async XLA Ops:
  7.2 81.0 %all-gather.5.cloned.1.call-start = ((), (), s32[]{:S(2)}) async-start(), calls=%async_computation.3 | async-start | bytes 2228224 | tf_op jit(solution)/shard_map/all_gather | solution.py:34
  7.9 119.5 %all-gather.3.cloned.1.call-start = ((), (), s32[]{:S(2)}) async-start(), calls=%async_computation.2 | async-start | bytes 2359296 | tf_op jit(solution)/shard_map/all_gather | solution.py:30
  53.6 184.6 %reduce-scatter.2.cloned.1.call-start = ((), (), s32[]{:S(2)}) async-start(), calls=%async_computation.4 | async-start | bytes 1310720 | tf_op jit(solution)/shard_map/reduce_scatter | solution.py:38
  127.4 4.5 %copy-start = (f32[128,512]{1,0:T(8,128)S(1)}, f32[128,512]{1,0:T(8,128)}, u32[]{:S(2)}) copy-start(f32[128,512]{1,0:T(8,128)} %param.7) | copy-start | bytes 786436
  127.4 124.4 %copy-start.4 = (f32[128]{0:T(128)S(1)}, f32[128]{0:T(128)}, u32[]{:S(2)}) copy-start(f32[128]{0:T(128)} %param.8) | copy-start | bytes 1540
  127.4 238.1 %copy-start.3 = (f32[512]{0:T(512)S(1)}, f32[512]{0:T(512)}, u32[]{:S(2)}) copy-start(f32[512]{0:T(512)} %param.9) | copy-start | bytes 6148
  251.8 157.6 %copy-start.2 = (f32[128]{0:T(128)}, f32[128]{0:T(128)S(1)}, u32[]{:S(2)}) copy-start(f32[128]{0:T(128)S(1)} %get-tuple-element.11) | copy-start | bytes 1540
  366.2 43.2 %copy-start.1 = (f32[512]{0:T(512)}, f32[512]{0:T(512)S(1)}, u32[]{:S(2)}) copy-start(f32[512]{0:T(512)S(1)} %get-tuple-element.9) | copy-start | bytes 6148
Sparse Core Ops, SparseCore 0:
  10.1 78.0 all-gather.4
  90.3 37.0 all-gather.2
  132.1 29.2 reduce-scatter.1
